TPU v7x, 128 devices: a whole 4x4x4 slice. The times are simulated.
128 devices in a mesh: section: 2 (over z_lo), dp: 16 (over y, z_hi, core), tensor: 4 (over x).
Axes of the slice: x: 4, y: 4, z: 4 (z_hi: 2, z_lo: 2; z = z_hi * 2 + z_lo), core: 2. Of those that a mesh axis runs over, the one named last changes fastest.
Arguments:
- hidden_parts: bfloat16 [2, 4, 512, 8192], P('section', None, 'dp'), may hold values from -1 to 1
- targets: int32 [4, 512], P(None, 'dp'), may hold values from 0 to 32767
- norm_gain: float32 [8192], replicated, may hold values from 0.1 to 1.9
- head_weight: bfloat16 [8192, 32768], P('dp', ('section', 'tensor')), may hold values from -0.1105957 to 0.1105957
Outputs:
- token_loss: float32 [4, 512], P(None, 'dp')
- hidden_grad: float32 [2, 4, 512, 8192], P('section', None, 'dp')
- head_grad: float32 [8192, 32768], P('dp', ('section', 'tensor'))
- gain_grad: float32 [16, 8192], P('dp')
All inputs are finite; a program needn't handle non-finite values.
Results may differ from a plain program's by a relative error of at most 0.0034.
Values may be sent and summed in bfloat16 or wider, within the bound.
No kernel may reach another device: no remote copies, remote signals or barrier semaphores. Data moves between devices by JAX's collectives and lax.ppermute only.
A program may use at most 128 MiB of HBM per device.

v0:
```python
import jax
import jax.numpy as jnp
from jax import lax
from jax.sharding import Mesh, PartitionSpec as P

NORM_EPS = 1e-05
CHUNKS = 2
ROW_SCALE = 2.0**17
HEAD_SCALE = 2.0**-3
BF16, F16, F32 = jnp.bfloat16, jnp.float16, jnp.float32


def shift(x, axis, step):
    size = lax.axis_size(axis)
    return lax.ppermute(x, axis, [((i + step) % size, i) for i in range(size)])


def flip(x, axes, bits):
    size = 1
    for axis in axes:
        size *= lax.axis_size(axis)
    return lax.ppermute(x, axes, [(i, i ^ bits) for i in range(size)])


def after(x, y):
    return lax.optimization_barrier((x, y))[0]


def merge(parts):
    top = parts[0][..., 0, :]
    for part in parts[1:]:
        top = jnp.maximum(top, part[..., 0, :])
    totals = [part[..., 1, :] * jnp.exp(part[..., 0, :] - top) for part in parts]
    hits = [part[..., 2, :] for part in parts]
    while len(totals) > 1:
        half = len(totals) // 2
        totals = [totals[i] + totals[i + half] for i in range(half)]
        hits = [hits[i] + hits[i + half] for i in range(half)]
    return jnp.stack([top, totals[0], hits[0]], axis=-2)


def swap(x, axis):
    return lax.all_to_all(x, axis, 0, 0, tiled=True)


def total(pieces):
    pieces = pieces.astype(F32)
    return (pieces[0] + pieces[2]) + (pieces[1] + pieces[3])


def local(hidden_parts, targets, norm_gain, head_weight):
    s, h, c, t = (lax.axis_index(name) for name in ("s", "h", "c", "t"))
    me = 2 * h + c
    rows, cols = head_weight.shape
    part = cols // 4
    width = 4 * rows
    batches, tok_count, features = hidden_parts.shape[1:]
    count = batches * tok_count
    size = count // CHUNKS
    quarter = size // 4
    eighth = quarter // 2

    pieces = [lax.dynamic_slice_in_dim(head_weight, (me ^ r) * part, part, 1) for r in range(4)]
    arrived = [pieces[0], flip(pieces[1], ("h", "c"), 1), flip(pieces[2], ("h", "c"), 2)]
    first_column = (me + 4 * (4 * s + t)) * part

    hidden = hidden_parts.reshape(CHUNKS, 4, quarter, features)
    own = lax.dynamic_index_in_dim(hidden, t, 1, keepdims=False).reshape(CHUNKS * quarter, features)
    mixed = own.astype(F32) + flip(own, ("s",), 1).astype(F32)
    radius = jnp.sqrt(jnp.mean(mixed * mixed, axis=-1, keepdims=True) + NORM_EPS)
    unit = mixed / radius
    normed = (norm_gain * unit).astype(BF16)
    over_y = swap(normed.reshape(CHUNKS * quarter, 4, width).transpose(1, 0, 2), "y")
    got = flip(after(over_y, arrived[2]), ("s", "h"), 3)
    arrived.append(flip(after(pieces[3], got), ("h", "c"), 3))
    blocks = jnp.stack(arrived)
    weight = jnp.concatenate([lax.dynamic_index_in_dim(blocks, me ^ a, 0, keepdims=False) for a in range(4)], axis=0)
    over_h = [
        jnp.stack([v.reshape(4, CHUNKS, quarter, width)[:, k] for v in (over_y, got)], axis=1) for k in range(CHUNKS)
    ]
    unit = unit.reshape(CHUNKS, 2, eighth, features)
    radius = radius.reshape(CHUNKS, 2, eighth, 1)

    ids = after(targets.reshape(count), got)
    ids = jnp.stack([ids, flip(ids, ("h",), 1)])
    ids = jnp.stack([ids, flip(ids, ("c",), 1)])

    def gather(k, wait):
        over_t = after(lax.all_gather(over_h[k], "t", axis=0), wait)
        over_c = jnp.stack([over_t, flip(over_t, ("c",), 1)]).transpose(2, 0, 1, 3, 4, 5)
        return lax.optimization_barrier(over_c.reshape(16 * size, width))

    def partial_logits(gathered):
        out = jnp.dot(gathered, weight, preferred_element_type=F32).astype(F16).reshape(4, 4 * size, part)
        return out, swap(out, "y")

    def loss_and_grad(k, pieces, before_last):
        logits = total(pieces)
        here = ids.reshape(2, 2, CHUNKS, 4, quarter)[:, :, k].transpose(0, 2, 1, 3).reshape(-1)
        is_target = lax.broadcasted_iota(jnp.int32, logits.shape, 1) == (here - first_column)[:, None]
        top = jnp.max(logits, axis=1)
        sums = jnp.sum(jnp.exp(logits - top[:, None]), axis=1)
        hit = jnp.sum(jnp.where(is_target, logits, 0.0), axis=1)
        stats = jnp.stack([v.reshape(2, 4, 2, quarter) for v in (top, sums, hit)], axis=3)
        stats = merge([stats, flip(stats, ("c",), 1)[::-1]])
        got = [flip(stats, ("s", "h"), r) for r in range(1, 4)]
        stats = merge([stats, got[0][:, :, ::-1], got[1], got[2][:, :, ::-1]])
        stats = after(stats, before_last)
        stats = merge([stats] + [shift(stats, "t", r) for r in range(1, 4)])
        log_total = stats[..., 0, :] + jnp.log(stats[..., 1, :])
        loss = log_total - stats[..., 2, :]
        grad = (jnp.exp(logits - log_total.reshape(-1)[:, None]) - is_target.astype(F32)).astype(BF16)
        return loss[0, :, 0].reshape(size), grad, lax.all_gather(grad, "y", axis=0, tiled=True)

    def row_product(grads):
        return lax.dot_general(grads, weight, (((1,), (1,)), ((), ())), preferred_element_type=F32) * ROW_SCALE

    def head_product(gathered, grads):
        return lax.dot_general(gathered, grads, (((0,), (0,)), ((), ())), preferred_element_type=F32)

    def over_cores(product, wait):
        product = product.reshape(4, 2, 2 * size, width)
        got = flip(after(product[:, 1].astype(F16), wait), ("c",), 1)
        return product[:, 0] + got.astype(F32)

    def over_tensor(kept):
        sent = kept.reshape(4, 4, 2 * quarter, width).transpose(1, 0, 2, 3).astype(F16)
        return swap(sent, "t")

    def over_z(pieces):
        kept = total(pieces).astype(F16).reshape(4, 2, 2, eighth, width)
        kept = jnp.where(h == 0, kept, kept[:, ::-1]).transpose(2, 1, 0, 3, 4)
        return swap(kept.reshape(4, 4, eighth, width), ("s", "h"))

    def to_owner(k, pieces):
        got = swap(total(pieces).astype(F16), "y")
        row_grads = got.transpose(1, 0, 2).reshape(eighth, features).astype(F32) * (1.0 / ROW_SCALE)
        u = lax.dynamic_index_in_dim(unit[k], s, 0, keepdims=False)
        scaled = norm_gain * row_grads
        hidden_grad = scaled - u * jnp.mean(scaled * u, axis=-1, keepdims=True)
        hidden_grad = hidden_grad / lax.dynamic_index_in_dim(radius[k], s, 0, keepdims=False)
        return hidden_grad.astype(BF16), jnp.sum(row_grads * u, axis=0, keepdims=True), got

    def in_order(everyone):
        everyone = everyone.reshape(2, 4, eighth, features).transpose(1, 0, 2, 3)
        return everyone.reshape(size, features).astype(F32)

    x0 = gather(0, (arrived[3], ids))
    part0, got0 = partial_logits(x0)
    x1 = gather(1, part0)
    part1, got1 = partial_logits(x1)
    loss0, grad0, grads0 = loss_and_grad(0, got0, part1)
    loss1, grad1, grads1 = loss_and_grad(1, after(got1, grad0), grad0)

    got_t0 = over_tensor(over_cores(row_product(grads0), part1))
    head0 = head_product(x0, after(grads0, grad1))
    got_z0 = over_z(got_t0)
    hid0, gain0, got_y0 = to_owner(0, got_z0)

    grads1 = after(grads1, (head0, got_t0))
    head = ((head0 + head_product(x1, grads1)) * HEAD_SCALE).astype(F16).reshape(4, rows, part)
    got_head = [lax.dynamic_index_in_dim(head, me ^ r, 0, keepdims=False) for r in range(4)]
    got_head = [got_head[0]] + [flip(after(got_head[r], got_z0), ("h", "c"), r) for r in range(1, 4)]
    kept1 = over_cores(row_product(after(grads1, (head, got_z0))), got_y0)
    got_t1 = over_tensor(kept1)
    hid1, gain1, _ = to_owner(1, over_z(after(got_t1, got_head[2:])))
    all0 = lax.all_gather(after(hid0, (got_head[2:], got_t1)), ("s", "t"))

    gain = gain0 + gain1
    upper = gain.astype(BF16)
    lower = (gain - upper.astype(F32)).astype(BF16)
    sent = jnp.concatenate([hid1, upper, lower], axis=0)
    all1 = lax.all_gather(sent, ("s", "t"))
    gain = jnp.sum(all1[:, eighth:].astype(F32), axis=(0, 1))[None]

    head_grad = jnp.zeros((rows, cols), F32)
    for r in range(4):
        piece = after(got_head[r], hid1).astype(F32) * (1.0 / HEAD_SCALE)
        head_grad = lax.dynamic_update_slice(head_grad, piece, (0, (me ^ r) * part))
    token_loss = jnp.concatenate([loss0, loss1]).reshape(batches, tok_count)
    hidden_grad = jnp.concatenate([in_order(all0), in_order(all1[:, :eighth])])
    return token_loss, hidden_grad.reshape(1, batches, tok_count, features), head_grad, gain


def solution(mesh):
    fine = Mesh(mesh.devices.reshape(2, 4, 2, 2, 4), ("s", "y", "h", "c", "t"))
    dp = ("y", "h", "c")
    in_specs = (P("s", None, dp, None), P(None, dp), P(), P(dp, ("s", "t")))
    out_specs = (P(None, dp), P("s", None, dp, None), P(dp, ("s", "t")), P(dp, None))
    return jax.shard_map(local, mesh=fine, in_specs=in_specs, out_specs=out_specs, check_vma=False)
```

profile of v0, /device:TPU:0, one launch (start us, length us, event | category | flops | bytes accessed | tf_op | source)
XLA Modules:
  0.0 508.3 jit_solution(2436377814142908423)
XLA Ops:
  18.4 5.2 %collective-permute-done = bf16[32,8192]{1,0:T(8,128)(2,1)S(1)} collective-permute-done((bf16[32,8192]{1,0:T(8,128)(2,1)S(1)}, bf16[32,8192]{1,0:T(8,128)(2,1)S(1)}, u32[]{:S(2)}, u32[]{:S(2)}) %collective-permute-start) | collective-permute-done | bytes 524320 | tf_op jit(solution)/shard_map/ppermute | solution.py:22
  25.9 12.4 %all_to_all.45 = bf16[4,32,2048]{2,1,0:T(8,128)(2,1)S(1)} all-to-all(bf16[4,32,2048]{2,1,0:T(8,128)(2,1)S(1)} %copy.42), channel_id=1, replica_groups=mesh['s'=2,'y'=4,'h'=2,'c'=2,'t'=4] {'y'}, dimensions={0} | all-to-all | bytes 1048576 | tf_op jit(solution)/shard_map/all_to_all | solution.py:43
  38.3 10.3 %collective-permute-done.1 = bf16[512,1024]{1,0:T(8,128)(2,1)} collective-permute-done((bf16[512,1024]{1,0:T(8,128)(2,1)}, bf16[512,1024]{1,0:T(8,128)(2,1)}, u32[]{:S(2)}, u32[]{:S(2)}) %collective-permute-start.1) | collective-permute-done | bytes 1048608 | tf_op jit(solution)/shard_map/ppermute | solution.py:22
  48.7 14.0 %collective-permute-done.2 = bf16[4,32,2048]{2,1,0:T(8,128)(2,1)S(1)} collective-permute-done((bf16[4,32,2048]{2,1,0:T(8,128)(2,1)S(1)}, bf16[4,32,2048]{2,1,0:T(8,128)(2,1)S(1)}, u32[]{:S(2)}, u32[]{:S(2)}) %collective-permute-start.2) | collective-permute-done | bytes 524320 | tf_op jit(solution)/shard_map/ppermute | solution.py:22
  63.7 25.5 %collective-permute-done.3 = bf16[512,1024]{1,0:T(8,128)(2,1)} collective-permute-done((bf16[512,1024]{1,0:T(8,128)(2,1)}, bf16[512,1024]{1,0:T(8,128)(2,1)}, u32[]{:S(2)}, u32[]{:S(2)}) %collective-permute-start.3) | collective-permute-done | bytes 1048608 | tf_op jit(solution)/shard_map/ppermute | solution.py:22
  105.6 5.7 %convolution_convert_fusion.1 = f16[1024,1024]{1,0:T(8,128)(2,1)} fusion(bf16[1024,2048]{1,0:T(8,128)(2,1)S(1)} %bitcast.302, bf16[512,1024]{1,0:T(8,128)(2,1)S(1)} %get-tuple-element.81, bf16[512,1024]{1,0:T(8,128)(2,1)S(1)} %get-tuple-element.82, bf16[512,1024]{1,0:T(8,128)(2,1)S(1)} %get-tuple-element.83, bf16[512,1024]{1,0:T(8,128)(2,1)S(1)} %get-tuple-element.80), kind=kOutput, calls=%fused_computation.23 | convolution fusion | flops 4312793088 | bytes 10485760 | tf_op jit(solution)/shard_map/dot_general | solution.py:94
  122.0 4.5 all-gather.18.cloned.1.call-done
  126.7 15.9 %all-to-all-done.1 = f16[4,256,1024]{2,1,0:T(8,128)(2,1)S(1)} async-done(((f16[4,256,1024]{2,1,0:T(8,128)(2,1)}), f16[4,256,1024]{2,1,0:T(8,128)(2,1)S(1)}, u32[]{:S(2)}, u32[]{:S(2)}) %all-to-all-start.1) | async-done | bytes 2097184 | tf_op jit(solution)/shard_map/all_to_all | solution.py:43
  159.4 5.7 %convolution_convert_fusion = f16[1024,1024]{1,0:T(8,128)(2,1)} fusion(bf16[1024,2048]{1,0:T(8,128)(2,1)S(1)} %bitcast.304, bf16[512,1024]{1,0:T(8,128)(2,1)S(1)} %copy-done.7, bf16[512,1024]{1,0:T(8,128)(2,1)S(1)} %copy-done.10, bf16[512,1024]{1,0:T(8,128)(2,1)S(1)} %copy-done.12, bf16[512,1024]{1,0:T(8,128)(2,1)S(1)} %get-tuple-element.80), kind=kOutput, calls=%fused_computation.22 | convolution fusion | flops 4312793088 | bytes 10485760 | tf_op jit(solution)/shard_map/dot_general | solution.py:94
  179.9 40.4 %all-to-all-done.2 = f16[4,256,1024]{2,1,0:T(8,128)(2,1)S(1)} async-done(((f16[4,256,1024]{2,1,0:T(8,128)(2,1)}), f16[4,256,1024]{2,1,0:T(8,128)(2,1)S(1)}, u32[]{:S(2)}, u32[]{:S(2)}) %all-to-all-start.2) | async-done | bytes 2097184 | tf_op jit(solution)/shard_map/all_to_all | solution.py:43
  222.0 6.7 %convolution_multiply_fusion.1 = f32[1024,2048]{1,0:T(8,128)S(1)} fusion(bf16[1024,1024]{1,0:T(8,128)(2,1)} %all-gather.12.cloned.1.call-done, bf16[512,1024]{1,0:T(8,128)(2,1)S(1)} %copy-done.8, bf16[512,1024]{1,0:T(8,128)(2,1)} %copy-done.9, bf16[512,1024]{1,0:T(8,128)(2,1)} %copy-done.11, bf16[512,1024]{1,0:T(8,128)(2,1)S(1)} %get-tuple-element.80), kind=kOutput, calls=%fused_computation.2 | convolution fusion | flops 4313841664 | bytes 14680064 | tf_op jit(solution)/shard_map/dot_general | solution.py:116
  261.6 10.8 %fusion.90 = f32[2048,1024]{1,0:T(8,128)} fusion(bf16[1024,2048]{1,0:T(8,128)(2,1)} %bitcast.303, bf16[1024,1024]{1,0:T(8,128)(2,1)} %all-gather.12.cloned.1.call-done), kind=kOutput, calls=%fused_computation.225 | convolution fusion | flops 4294967296 | bytes 14680064 | tf_op jit(solution)/shard_map/dot_general | solution.py:119
  272.4 13.0 %all-to-all-done.3 = f16[4,4,32,2048]{3,2,1,0:T(8,128)(2,1)S(1)} async-done(((f16[4,4,32,2048]{3,2,1,0:T(8,128)(2,1)}), f16[4,4,32,2048]{3,2,1,0:T(8,128)(2,1)S(1)}, u32[]{:S(2)}, u32[]{:S(2)}) %all-to-all-start.3) | async-done | bytes 2097184 | tf_op jit(solution)/shard_map/all_to_all | solution.py:43
  290.8 12.1 %multiply_convert_fusion = f16[2048,1024]{1,0:T(8,128)(2,1)} fusion(f32[2048,1024]{1,0:T(8,128)} %fusion.90, bf16[1024,2048]{1,0:T(8,128)(2,1)} %bitcast.305, bf16[1024,1024]{1,0:T(8,128)(2,1)} %all-gather.14.cloned.1.call-done), kind=kOutput, calls=%fused_computation | convolution fusion | flops 4301258752 | bytes 18874368 | tf_op jit(solution)/shard_map/dot_general | solution.py:119
  307.1 7.5 %convolution_multiply_fusion = f32[1024,2048]{1,0:T(8,128)S(1)} fusion(bf16[1024,1024]{1,0:T(8,128)(2,1)} %all-gather.14.cloned.1.call-done, bf16[512,1024]{1,0:T(8,128)(2,1)} %copy-done.6, bf16[512,1024]{1,0:T(8,128)(2,1)} %copy-done.9, bf16[512,1024]{1,0:T(8,128)(2,1)} %copy-done.11, bf16[512,1024]{1,0:T(8,128)(2,1)S(1)} %get-tuple-element.80), kind=kOutput, calls=%fused_computation.1 | convolution fusion | flops 4313841664 | bytes 14680064 | tf_op jit(solution)/shard_map/dot_general | solution.py:116
  330.7 4.8 dynamic-slice_bitcast_fusion
  339.2 24.0 %collective-permute-done.24 = f16[512,1024]{1,0:T(8,128)(2,1)} collective-permute-done((f16[512,1024]{1,0:T(8,128)(2,1)}, f16[512,1024]{1,0:T(8,128)(2,1)}, u32[]{:S(2)}, u32[]{:S(2)}) %collective-permute-start.24) | collective-permute-done | bytes 1048608 | tf_op jit(solution)/shard_map/ppermute | solution.py:22
  363.3 21.4 %collective-permute-done.25 = f16[512,1024]{1,0:T(8,128)(2,1)} collective-permute-done((f16[512,1024]{1,0:T(8,128)(2,1)}, f16[512,1024]{1,0:T(8,128)(2,1)}, u32[]{:S(2)}, u32[]{:S(2)}) %collective-permute-start.25) | collective-permute-done | bytes 1048608 | tf_op jit(solution)/shard_map/ppermute | solution.py:22
  392.9 7.8 %all-to-all-done.7 = f16[4,4,8,2048]{3,2,1,0:T(8,128)(2,1)S(1)} async-done(((f16[4,4,8,2048]{3,2,1,0:T(8,128)(2,1)}), f16[4,4,8,2048]{3,2,1,0:T(8,128)(2,1)S(1)}, u32[]{:S(2)}, u32[]{:S(2)}) %all-to-all-start.7) | async-done | bytes 524320 | tf_op jit(solution)/shard_map/all_to_all | solution.py:43
  401.5 4.7 all-to-all-start.8
  407.4 4.7 all-to-all-done.8
  421.4 4.4 broadcast_in_dim.10
  434.7 17.8 %all-gather.20.cloned.1.call-done = bf16[64,8192]{1,0:T(8,128)(2,1)} async-done(((bf16[8,8192]{1,0:T(8,128)(2,1)}), bf16[64,8192]{1,0:T(8,128)(2,1)}) %all-gather.20.cloned.1.call-update) | async-done | bytes 1048592 | tf_op jit(solution)/shard_map/all_gather | solution.py:167
  453.8 41.2 %all-gather.22.cloned.1.call-done = bf16[8,10,8192]{2,1,0:T(8,128)(2,1)} async-done(((bf16[1,10,8192]{2,1,0:T(8,128)(2,1)}), bf16[8,10,8192]{2,1,0:T(8,128)(2,1)}) %all-gather.22.cloned.1.call-update) | async-done | bytes 1310736 | tf_op jit(solution)/shard_map/all_gather | solution.py:173
  (261 shorter events, 172.5 us)
Async XLA Ops:
  7.2 86.3 %all-gather.16.cloned.1.call-start = ((), (), s32[]{:S(2)}) async-start(), calls=%async_computation.11 | async-start | bytes 2621440 | tf_op jit(solution)/shard_map/all_gather | solution.py:89
  8.8 14.9 %collective-permute-start = (bf16[32,8192]{1,0:T(8,128)(2,1)S(1)}, bf16[32,8192]{1,0:T(8,128)(2,1)S(1)}, u32[]{:S(2)}, u32[]{:S(2)}) collective-permute-start(bf16[32,8192]{1,0:T(8,128)(2,1)S(1)} %bitcast.300), channel_id=1, source_target_pairs={{0,64},{64,0},{1,65},{65,1},{2,66},{66,2},{3,67},{67,3},{4,68},{68... | collective-permute-start | bytes 1572872 | tf_op jit(solution)/shard_map/ppermute | solution.py:22
  14.8 33.8 %collective-permute-start.1 = (bf16[512,1024]{1,0:T(8,128)(2,1)}, bf16[512,1024]{1,0:T(8,128)(2,1)}, u32[]{:S(2)}, u32[]{:S(2)}) collective-permute-start(bf16[512,1024]{1,0:T(8,128)(2,1)} %get-tuple-element.86), channel_id=1, source_target_pairs={{0,8},{4,12},{8,0},{12,4},{1,9},{5,13},{9,1},{13,5},{2,10},{6,14},... | collective-permute-start | bytes 3145736 | tf_op jit(solution)/shard_map/ppermute | solution.py:22
  48.7 14.0 %collective-permute-start.2 = (bf16[4,32,2048]{2,1,0:T(8,128)(2,1)S(1)}, bf16[4,32,2048]{2,1,0:T(8,128)(2,1)S(1)}, u32[]{:S(2)}, u32[]{:S(2)}) collective-permute-start(bf16[4,32,2048]{2,1,0:T(8,128)(2,1)S(1)} %all_to_all.45), channel_id=1, source_target_pairs={{0,72},{8,64},{64,8},{72,0},{1,73},{9,65},{65,9},{73,1},{2,74},{10... | collective-permute-start | bytes 1572872 | tf_op jit(solution)/shard_map/ppermute | solution.py:22
  63.6 63.0 %all-gather.18.cloned.1.call-start = ((), (), s32[]{:S(2)}) async-start(), calls=%async_computation.12 | async-start | bytes 2621440 | tf_op jit(solution)/shard_map/all_gather | solution.py:89
  63.6 25.6 %collective-permute-start.3 = (bf16[512,1024]{1,0:T(8,128)(2,1)}, bf16[512,1024]{1,0:T(8,128)(2,1)}, u32[]{:S(2)}, u32[]{:S(2)}) collective-permute-start(bf16[512,1024]{1,0:T(8,128)(2,1)} %get-tuple-element.27), channel_id=1, source_target_pairs={{0,12},{4,8},{8,4},{12,0},{1,13},{5,9},{9,5},{13,1},{2,14},{6,10},... | collective-permute-start | bytes 3145736 | tf_op jit(solution)/shard_map/ppermute | solution.py:22
  111.3 31.3 %all-to-all-start.1 = ((f16[4,256,1024]{2,1,0:T(8,128)(2,1)}), f16[4,256,1024]{2,1,0:T(8,128)(2,1)S(1)}, u32[]{:S(2)}, u32[]{:S(2)}) async-start(f16[4,256,1024]{2,1,0:T(8,128)(2,1)} %bitcast.316), calls=%async_computation.1 | async-start | bytes 4194304 | tf_op jit(solution)/shard_map/all_to_all | solution.py:43
  115.7 106.2 %all-gather.12.cloned.1.call-start = ((), (), s32[]{:S(2)}) async-start(), calls=%async_computation.9 | async-start | bytes 2621440 | tf_op jit(solution)/shard_map/all_gather | solution.py:113
  126.6 27.6 %collective-permute-start.12 = (bf16[4,4,2,16,2048]{4,3,2,1,0:T(8,128)(2,1)}, bf16[4,4,2,16,2048]{4,3,2,1,0:T(8,128)(2,1)}, u32[]{:S(2)}, u32[]{:S(2)}) collective-permute-start(bf16[4,4,2,16,2048]{4,3,2,1,0:T(8,128)(2,1)} %bitcast.319), channel_id=1, source_target_pairs={{0,4},{4,0},{1,5},{5,1},{2,6},{6,2},{3,7},{7,3},{8,12},{12,8},{9,1... | collective-permute-start | bytes 6291464 | tf_op jit(solution)/shard_map/ppermute | solution.py:22
  176.2 44.1 %all-to-all-start.2 = ((f16[4,256,1024]{2,1,0:T(8,128)(2,1)}), f16[4,256,1024]{2,1,0:T(8,128)(2,1)S(1)}, u32[]{:S(2)}, u32[]{:S(2)}) async-start(f16[4,256,1024]{2,1,0:T(8,128)(2,1)} %bitcast.315), calls=%async_computation.2 | async-start | bytes 4194304 | tf_op jit(solution)/shard_map/all_to_all | solution.py:43
  179.8 111.0 %all-gather.14.cloned.1.call-start = ((), (), s32[]{:S(2)}) async-start(), calls=%async_computation.10 | async-start | bytes 2621440 | tf_op jit(solution)/shard_map/all_gather | solution.py:113
  221.8 11.8 %collective-permute-start.16 = (f32[2,4,2,3,16]{4,2,1,0,3:T(2,128)S(1)}, f32[2,4,2,3,16]{4,2,1,0,3:T(2,128)S(1)}, u32[]{:S(2)}, u32[]{:S(2)}) collective-permute-start(f32[2,4,2,3,16]{4,2,1,0,3:T(2,128)S(1)} %pad_maximum_fusion.8), channel_id=1, source_target_pairs={{0,4},{4,0},{1,5},{5,1},{2,6},{6,2},{3,7},{7,3},{8,12},{12,8},{9,1... | collective-permute-start | bytes 9224 | tf_op jit(solution)/shard_map/ppermute | solution.py:22
  233.3 18.9 %collective-permute-start.23 = (f16[4,128,2048]{2,1,0:T(8,128)(2,1)}, f16[4,128,2048]{2,1,0:T(8,128)(2,1)}, u32[]{:S(2)}, u32[]{:S(2)}) collective-permute-start(f16[4,128,2048]{2,1,0:T(8,128)(2,1)} %fusion.4), channel_id=1, source_target_pairs={{0,4},{4,0},{1,5},{5,1},{2,6},{6,2},{3,7},{7,3},{8,12},{12,8},{9,1... | collective-permute-start | bytes 6291464 | tf_op jit(solution)/shard_map/ppermute | solution.py:22
  257.9 27.4 %all-to-all-start.3 = ((f16[4,4,32,2048]{3,2,1,0:T(8,128)(2,1)}), f16[4,4,32,2048]{3,2,1,0:T(8,128)(2,1)S(1)}, u32[]{:S(2)}, u32[]{:S(2)}) async-start(f16[4,4,32,2048]{3,2,1,0:T(8,128)(2,1)} %copy.49), calls=%async_computation.3 | async-start | bytes 4194304 | tf_op jit(solution)/shard_map/all_to_all | solution.py:43
  287.1 15.8 %all-to-all-start.4 = ((f16[4,4,8,2048]{3,2,1,0:T(8,128)(2,1)}), f16[4,4,8,2048]{3,2,1,0:T(8,128)(2,1)S(1)}, u32[]{:S(2)}, u32[]{:S(2)}) async-start(f16[4,4,8,2048]{3,2,1,0:T(8,128)(2,1)} %bitcast.58), calls=%async_computation.4 | async-start | bytes 1048576 | tf_op jit(solution)/shard_map/all_to_all | solution.py:43
  303.7 14.0 %all-to-all-start.5 = ((f16[4,8,2048]{2,1,0:T(8,128)(2,1)}), f16[4,8,2048]{2,1,0:T(8,128)(2,1)S(1)}, u32[]{:S(2)}, u32[]{:S(2)}) async-start(f16[4,8,2048]{2,1,0:T(8,128)(2,1)} %fusion.41), calls=%async_computation.5 | async-start | bytes 262144 | tf_op jit(solution)/shard_map/all_to_all | solution.py:43
  327.1 57.6 %all-to-all-start.6 = ((f16[4,4,32,2048]{3,2,1,0:T(8,128)(2,1)}), f16[4,4,32,2048]{3,2,1,0:T(8,128)(2,1)S(1)}, u32[]{:S(2)}, u32[]{:S(2)}) async-start(f16[4,4,32,2048]{3,2,1,0:T(8,128)(2,1)} %copy.53), calls=%async_computation.6 | async-start | bytes 4194304 | tf_op jit(solution)/shard_map/all_to_all | solution.py:43
  335.5 27.8 %collective-permute-start.24 = (f16[512,1024]{1,0:T(8,128)(2,1)}, f16[512,1024]{1,0:T(8,128)(2,1)}, u32[]{:S(2)}, u32[]{:S(2)}) collective-permute-start(f16[512,1024]{1,0:T(8,128)(2,1)} %get-tuple-element.37), channel_id=1, source_target_pairs={{0,8},{4,12},{8,0},{12,4},{1,9},{5,13},{9,1},{13,5},{2,10},{6,14},... | collective-permute-start | bytes 3145736 | tf_op jit(solution)/shard_map/ppermute | solution.py:22
  339.0 45.7 %collective-permute-start.25 = (f16[512,1024]{1,0:T(8,128)(2,1)}, f16[512,1024]{1,0:T(8,128)(2,1)}, u32[]{:S(2)}, u32[]{:S(2)}) collective-permute-start(f16[512,1024]{1,0:T(8,128)(2,1)} %get-tuple-element.38), channel_id=1, source_target_pairs={{0,12},{4,8},{8,4},{12,0},{1,13},{5,9},{9,5},{13,1},{2,14},{6,10},... | collective-permute-start | bytes 3145736 | tf_op jit(solution)/shard_map/ppermute | solution.py:22
  386.5 14.2 %all-to-all-start.7 = ((f16[4,4,8,2048]{3,2,1,0:T(8,128)(2,1)}), f16[4,4,8,2048]{3,2,1,0:T(8,128)(2,1)S(1)}, u32[]{:S(2)}, u32[]{:S(2)}) async-start(f16[4,4,8,2048]{3,2,1,0:T(8,128)(2,1)} %bitcast.78), calls=%async_computation.7 | async-start | bytes 1048576 | tf_op jit(solution)/shard_map/all_to_all | solution.py:43
  401.5 10.7 %all-to-all-start.8 = ((f16[4,8,2048]{2,1,0:T(8,128)(2,1)}), f16[4,8,2048]{2,1,0:T(8,128)(2,1)S(1)}, u32[]{:S(2)}, u32[]{:S(2)}) async-start(f16[4,8,2048]{2,1,0:T(8,128)(2,1)} %fusion.42), calls=%async_computation.8 | async-start | bytes 262144 | tf_op jit(solution)/shard_map/all_to_all | solution.py:43
  406.2 46.3 %all-gather.20.cloned.1.call-start = ((), (), s32[]{:S(2)}) async-start(), calls=%async_computation.13 | async-start | bytes 1179648 | tf_op jit(solution)/shard_map/all_gather | solution.py:167
  407.4 14.0 %collective-permute-start.27 = (f16[512,1024]{1,0:T(8,128)(2,1)}, f16[512,1024]{1,0:T(8,128)(2,1)S(1)}, u32[]{:S(2)}, u32[]{:S(2)}) collective-permute-start(f16[512,1024]{1,0:T(8,128)(2,1)} %get-tuple-element.44), channel_id=1, source_target_pairs={{0,4},{4,0},{8,12},{12,8},{1,5},{5,1},{9,13},{13,9},{2,6},{6,2},{1... | collective-permute-start | bytes 3145736 | tf_op jit(solution)/shard_map/ppermute | solution.py:22
  415.3 79.6 %all-gather.22.cloned.1.call-start = ((), (), s32[]{:S(2)}) async-start(), calls=%async_computation.14 | async-start | bytes 2359296 | tf_op jit(solution)/shard_map/all_gather | solution.py:173
  (38 other events, 291.6 us)
Sparse Core Ops, SparseCore 0:
  63.7 29.6 all-gather.15
  95.7 30.8 all-gather.17
  176.3 41.6 all-gather.11
  252.3 26.5 all-gather.13
  415.5 36.9 all-gather.19
  454.5 40.3 all-gather.21
where the time goes:
time: 517 us; the launch traced here: 508 us
  waiting for transfers between devices  279 us (54%)
  starting transfers between devices  61.1 us (12%)
  other arithmetic  50.6 us (10%)
  matrix products  48.5 us (9%)
  local copies, waits for them, and re-layouts  41.4 us (8%)
  between operations  15.3 us (3%)
  blocking collectives  12.4 us (2%)
    ppermute x22, waiting for transfers between devices, flip(): return lax.ppermute(x, axes, [(i, i ^ bits) for i in range(size)])  119 us
    all_to_all x8, waiting for transfers between devices, swap(): return lax.all_to_all(x, axis, 0, 0, tiled=True)  81.7 us
    all_gather x1, waiting for transfers between devices, local(): all1 = lax.all_gather(sent, ('s', 't'))  41.2 us
    all_to_all x8, starting transfers between devices, swap(): return lax.all_to_all(x, axis, 0, 0, tiled=True)  31.2 us
    dot_general x2, matrix products, head_product(): lax.dot_general(gathered, grads, (((0,), (0,)), ((), ())), preferred_elem...  22.9 us
    ppermute x22, starting transfers between devices, flip(): return lax.ppermute(x, axes, [(i, i ^ bits) for i in range(size)])  22.6 us
    all_gather x1, waiting for transfers between devices, local(): all0 = lax.all_gather(after(hid0, (got_head[2:], got_t1)), ('s', 't'))  17.8 us
    dot_general x2, matrix products, row_product(): lax.dot_general(grads, weight, (((1,), (1,)), ((), ())), preferred_elemen...  14.2 us
  transfers between devices with their start and end apart: 42, of which 28 were waited for; matrix products, arithmetic and copies ran while one was open for 21% of the time, Pallas kernels for 0%

commit v1 on v0

--- a/solution.py
+++ b/solution.py
@@ -43,13 +43,17 @@
     return lax.all_to_all(x, axis, 0, 0, tiled=True)
 
 
+def pick(pieces, index):
+    return lax.dynamic_index_in_dim(jnp.stack(pieces), index, 0, keepdims=False)
+
+
 def total(pieces):
     pieces = pieces.astype(F32)
     return (pieces[0] + pieces[2]) + (pieces[1] + pieces[3])
 
 
 def local(hidden_parts, targets, norm_gain, head_weight):
-    s, h, c, t = (lax.axis_index(name) for name in ("s", "h", "c", "t"))
+    s, y, h, c, t = (lax.axis_index(name) for name in ("s", "y", "h", "c", "t"))
     me = 2 * h + c
     rows, cols = head_weight.shape
     part = cols // 4
@@ -61,7 +65,9 @@
     eighth = quarter // 2
 
     pieces = [lax.dynamic_slice_in_dim(head_weight, (me ^ r) * part, part, 1) for r in range(4)]
-    arrived = [pieces[0], flip(pieces[1], ("h", "c"), 1), flip(pieces[2], ("h", "c"), 2)]
+    early = 3 * rows // 4
+    arrived = [pieces[0], flip(pieces[1], ("h", "c"), 1)]
+    first = flip(pieces[2][:early], ("h", "c"), 2)
     first_column = (me + 4 * (4 * s + t)) * part
 
     hidden = hidden_parts.reshape(CHUNKS, 4, quarter, features)
@@ -71,7 +77,9 @@
     unit = mixed / radius
     normed = (norm_gain * unit).astype(BF16)
     over_y = swap(normed.reshape(CHUNKS * quarter, 4, width).transpose(1, 0, 2), "y")
-    got = flip(after(over_y, arrived[2]), ("s", "h"), 3)
+    got = flip(after(over_y, first), ("s", "h"), 3)
+    second = flip(after(pieces[2][early:], got), ("h", "c"), 2)
+    arrived.append(jnp.concatenate([first, second]))
     arrived.append(flip(after(pieces[3], got), ("h", "c"), 3))
     blocks = jnp.stack(arrived)
     weight = jnp.concatenate([lax.dynamic_index_in_dim(blocks, me ^ a, 0, keepdims=False) for a in range(4)], axis=0)
@@ -113,72 +121,95 @@
         return loss[0, :, 0].reshape(size), grad, lax.all_gather(grad, "y", axis=0, tiled=True)
 
     def row_product(grads):
-        return lax.dot_general(grads, weight, (((1,), (1,)), ((), ())), preferred_element_type=F32) * ROW_SCALE
+        ordered = grads.reshape(4, 2, 4, 2 * quarter, part).transpose(1, 2, 0, 3, 4).reshape(2, 8 * size, part)
+        dims = (((1,), (1,)), ((), ()))
+        kept, sent = (lax.dot_general(g, weight, dims, preferred_element_type=F32) * ROW_SCALE for g in ordered)
+        return kept, sent.astype(F16)
 
     def head_product(gathered, grads):
         return lax.dot_general(gathered, grads, (((0,), (0,)), ((), ())), preferred_element_type=F32)
 
-    def over_cores(product, wait):
-        product = product.reshape(4, 2, 2 * size, width)
-        got = flip(after(product[:, 1].astype(F16), wait), ("c",), 1)
-        return product[:, 0] + got.astype(F32)
+    def over_cores(products, wait):
+        kept, sent = products
+        return (kept + flip(after(sent, wait), ("c",), 1).astype(F32)).astype(F16)
 
     def over_tensor(kept):
-        sent = kept.reshape(4, 4, 2 * quarter, width).transpose(1, 0, 2, 3).astype(F16)
-        return swap(sent, "t")
+        return swap(kept.reshape(4, 4, 2 * quarter, width), "t")
 
     def over_z(pieces):
-        kept = total(pieces).astype(F16).reshape(4, 2, 2, eighth, width)
-        kept = jnp.where(h == 0, kept, kept[:, ::-1]).transpose(2, 1, 0, 3, 4)
-        return swap(kept.reshape(4, 4, eighth, width), ("s", "h"))
-
-    def to_owner(k, pieces):
-        got = swap(total(pieces).astype(F16), "y")
-        row_grads = got.transpose(1, 0, 2).reshape(eighth, features).astype(F32) * (1.0 / ROW_SCALE)
+        kept = total(pieces).reshape(4, 2, 2, eighth, width)
+        mine = lax.dynamic_index_in_dim(kept, s, 2, keepdims=False)
+        other = lax.dynamic_index_in_dim(kept, 1 - s, 2, keepdims=False).astype(F16)
+        got = [
+            flip(mine[:, 1].astype(F16), ("s", "h"), 1),
+            flip(other[:, 0], ("s", "h"), 2),
+            flip(other[:, 1], ("s", "h"), 3),
+        ]
+        return (mine[:, 0] + got[0].astype(F32)) + (got[1].astype(F32) + got[2].astype(F32)), got
+
+    def to_owner(k, summed):
+        sent = summed.astype(F16)
+        sent = [lax.dynamic_index_in_dim(sent, (y + r) % 4, 0, keepdims=False) for r in range(4)]
+        got = [shift(sent[4 - r], "y", r) for r in range(1, 4)]
+        blocks = [sent[0]] + got
+        row_grads = jnp.concatenate([pick(blocks, (b - y) % 4) for b in range(4)], axis=1).astype(F32) * (1.0 / ROW_SCALE)
         u = lax.dynamic_index_in_dim(unit[k], s, 0, keepdims=False)
         scaled = norm_gain * row_grads
         hidden_grad = scaled - u * jnp.mean(scaled * u, axis=-1, keepdims=True)
         hidden_grad = hidden_grad / lax.dynamic_index_in_dim(radius[k], s, 0, keepdims=False)
         return hidden_grad.astype(BF16), jnp.sum(row_grads * u, axis=0, keepdims=True), got
 
-    def in_order(everyone):
-        everyone = everyone.reshape(2, 4, eighth, features).transpose(1, 0, 2, 3)
-        return everyone.reshape(size, features).astype(F32)
+    def in_order(mine, got):
+        return jnp.stack([pick([mine, got], a ^ s) for a in range(2)]).reshape(quarter, features)
+
+    def halves(v):
+        upper = v.astype(BF16)
+        return [upper, (v - upper.astype(F32)).astype(BF16)]
+
+    def whole(rows):
+        return rows[-2:-1].astype(F32) + rows[-1:].astype(F32)
 
     x0 = gather(0, (arrived[3], ids))
     part0, got0 = partial_logits(x0)
     x1 = gather(1, part0)
     part1, got1 = partial_logits(x1)
-    loss0, grad0, grads0 = loss_and_grad(0, got0, part1)
-    loss1, grad1, grads1 = loss_and_grad(1, after(got1, grad0), grad0)
-
-    got_t0 = over_tensor(over_cores(row_product(grads0), part1))
+    loss0, grad0, grads0 = loss_and_grad(0, got0, got1)
+    products0 = row_product(grads0)
+    loss1, grad1, grads1 = loss_and_grad(1, after(got1, grad0), products0[1])
+
+    kept0 = over_cores(products0, part1)
+    got_t0 = over_tensor(kept0)
     head0 = head_product(x0, after(grads0, grad1))
-    got_z0 = over_z(got_t0)
-    hid0, gain0, got_y0 = to_owner(0, got_z0)
-
-    grads1 = after(grads1, (head0, got_t0))
-    head = ((head0 + head_product(x1, grads1)) * HEAD_SCALE).astype(F16).reshape(4, rows, part)
+    summed0, got_z0 = over_z(got_t0)
+    hid0, gain0, got_y0 = to_owner(0, summed0)
+
+    grads1 = after(grads1, (head0, kept0))
+    products1 = row_product(grads1)
+    got_t1 = over_tensor(over_cores(products1, got0))
+    head = head0 + head_product(x1, after(grads1, (products1[1], got_t0)))
+    head = (head * HEAD_SCALE).astype(F16).reshape(4, rows, part)
     got_head = [lax.dynamic_index_in_dim(head, me ^ r, 0, keepdims=False) for r in range(4)]
     got_head = [got_head[0]] + [flip(after(got_head[r], got_z0), ("h", "c"), r) for r in range(1, 4)]
-    kept1 = over_cores(row_product(after(grads1, (head, got_z0))), got_y0)
-    got_t1 = over_tensor(kept1)
-    hid1, gain1, _ = to_owner(1, over_z(after(got_t1, got_head[2:])))
-    all0 = lax.all_gather(after(hid0, (got_head[2:], got_t1)), ("s", "t"))
-
-    gain = gain0 + gain1
-    upper = gain.astype(BF16)
-    lower = (gain - upper.astype(F32)).astype(BF16)
-    sent = jnp.concatenate([hid1, upper, lower], axis=0)
-    all1 = lax.all_gather(sent, ("s", "t"))
-    gain = jnp.sum(all1[:, eighth:].astype(F32), axis=(0, 1))[None]
+    summed1, _ = over_z(after(got_t1, got_head[2:]))
+    pair0 = flip(after(hid0, (got_head[2:], got_t1)), ("s",), 1)
+    whole0 = in_order(hid0, pair0)
+    all0 = lax.all_gather(whole0, "t", axis=0, tiled=True)
+    hid1, gain1, _ = to_owner(1, after(summed1, pair0))
+
+    sent1 = jnp.concatenate([hid1] + halves(gain0 + gain1), axis=0)
+    pair1 = flip(after(sent1, whole0), ("s",), 1)
+    whole1 = in_order(hid1, pair1[:eighth])
+    whole1 = jnp.concatenate([whole1] + halves(whole(sent1) + whole(pair1)), axis=0)
+    all1 = [whole1] + [shift(whole1, "t", r) for r in range(1, 4)]
+    gain = (whole(all1[0]) + whole(all1[2])) + (whole(all1[1]) + whole(all1[3]))
+    all1 = jnp.concatenate([pick([v[:quarter] for v in all1], (a - t) % 4) for a in range(4)], axis=0)
 
     head_grad = jnp.zeros((rows, cols), F32)
     for r in range(4):
-        piece = after(got_head[r], hid1).astype(F32) * (1.0 / HEAD_SCALE)
+        piece = after(got_head[r], pair1).astype(F32) * (1.0 / HEAD_SCALE)
         head_grad = lax.dynamic_update_slice(head_grad, piece, (0, (me ^ r) * part))
     token_loss = jnp.concatenate([loss0, loss1]).reshape(batches, tok_count)
-    hidden_grad = jnp.concatenate([in_order(all0), in_order(all1[:, :eighth])])
+    hidden_grad = jnp.concatenate([all0, all1]).astype(F32)
     return token_loss, hidden_grad.reshape(1, batches, tok_count, features), head_grad, gain
 
 

time: 517 us -> 440 us (0.85)
  waiting for transfers between devices: 279 us -> 192 us
  starting transfers between devices: 61.1 us -> 83.4 us
  blocking collectives: 12.4 us -> 0 us
  matrix products: 48.5 us -> 60.6 us
  other arithmetic: 50.6 us -> 41.3 us
    all_gather x2 -> x1, waiting for transfers between devices: 59 us -> 0.01 us  [local(): all0 = lax.all_gather(whole0, 't', axis=0, tiled=True)]
    all_to_all x8 -> x5, waiting for transfers between devices: 81.7 us -> 35.7 us  [swap(): return lax.all_to_all(x, axis, 0, 0, tiled=True)]
    all_gather x2, waiting for transfers between devices: 0.04 us -> 24.6 us  [loss_and_grad(): lax.all_gather(grad, 'y', axis=0, tiled=True)]
    ppermute x6 -> x15, starting transfers between devices: 7.17 us -> 24.8 us  [shift(): return lax.ppermute(x, axis, [((i + step) % size, i) for i in range(size)])]
    ppermute x22 -> x31, starting transfers between devices: 22.6 us -> 37.4 us  [flip(): return lax.ppermute(x, axes, [(i, i ^ bits) for i in range(size)])]
    dot_general x2 -> x4, matrix products: 14.2 us -> 28.9 us  [row_product(): lax.dot_general(g, weight, dims, preferred_element_type=F32) * ROW_SCALE]
    all_to_all x1 -> x0, blocking collectives: 12.4 us -> none  [swap(): return lax.all_to_all(x, axis, 0, 0, tiled=True)]
    all_to_all x8 -> x5, starting transfers between devices: 31.2 us -> 21.2 us  [swap(): return lax.all_to_all(x, axis, 0, 0, tiled=True)]
  transfers between devices with their start and end apart: 42 -> 56, of which waited for: 28 -> 35; matrix products, arithmetic and copies ran while one was open for 21% -> 25% of each run, Pallas kernels for 0% -> 0%
where the time goes in v1:
time: 440 us; the launch traced here: 432 us
  waiting for transfers between devices  192 us (44%)
  starting transfers between devices  83.4 us (19%)
  matrix products  60.6 us (14%)
  other arithmetic  41.3 us (9%)
  local copies, waits for them, and re-layouts  40 us (9%)
  between operations  15.2 us (3%)
    ppermute x31, waiting for transfers between devices, flip(): return lax.ppermute(x, axes, [(i, i ^ bits) for i in range(size)])  111 us
    ppermute x31, starting transfers between devices, flip(): return lax.ppermute(x, axes, [(i, i ^ bits) for i in range(size)])  37.4 us
    all_to_all x5, waiting for transfers between devices, swap(): return lax.all_to_all(x, axis, 0, 0, tiled=True)  35.7 us
    dot_general x4, matrix products, row_product(): lax.dot_general(g, weight, dims, preferred_element_type=F32) * ROW_SCALE  28.9 us
    ppermute x15, starting transfers between devices, shift(): return lax.ppermute(x, axis, [((i + step) % size, i) for i in range(size)])  24.8 us
    all_gather x2, waiting for transfers between devices, loss_and_grad(): lax.all_gather(grad, 'y', axis=0, tiled=True)  24.6 us
    all_to_all x5, starting transfers between devices, swap(): return lax.all_to_all(x, axis, 0, 0, tiled=True)  21.2 us
    dot_general x2, matrix products, head_product(): lax.dot_general(gathered, grads, (((0,), (0,)), ((), ())), preferred_elem...  18.1 us
  transfers between devices with their start and end apart: 56, of which 35 were waited for; matrix products, arithmetic and copies ran while one was open for 25% of the time, Pallas kernels for 0%

profile of v1, /device:TPU:0, one launch (start us, length us, event | category | flops | bytes accessed | tf_op | source)
XLA Modules:
  0.0 432.2 jit_solution(18330892753240797788)
XLA Ops:
  15.7 7.9 %collective-permute-done = bf16[32,8192]{1,0:T(8,128)(2,1)S(1)} collective-permute-done((bf16[32,8192]{1,0:T(8,128)(2,1)S(1)}, bf16[32,8192]{1,0:T(8,128)(2,1)S(1)}, u32[]{:S(2)}, u32[]{:S(2)}) %collective-permute-start) | collective-permute-done | bytes 524320 | tf_op jit(solution)/shard_map/ppermute | solution.py:22
  27.4 4.6 %all-to-all-start = ((bf16[4,32,2048]{2,1,0:T(8,128)(2,1)}), bf16[4,32,2048]{2,1,0:T(8,128)(2,1)S(1)}, u32[]{:S(2)}, u32[]{:S(2)}) async-start(bf16[4,32,2048]{2,1,0:T(8,128)(2,1)} %copy.44), calls=%async_computation | async-start | bytes 1048576 | tf_op jit(solution)/shard_map/all_to_all | solution.py:43
  32.0 11.0 %collective-permute-done.1 = bf16[384,1024]{1,0:T(8,128)(2,1)S(1)} collective-permute-done((bf16[384,1024]{1,0:T(8,128)(2,1)S(1)}, bf16[384,1024]{1,0:T(8,128)(2,1)S(1)}, u32[]{:S(2)}, u32[]{:S(2)}) %collective-permute-start.1) | collective-permute-done | bytes 786464 | tf_op jit(solution)/shard_map/ppermute | solution.py:22
  44.2 12.8 %collective-permute-done.2 = bf16[4,32,2048]{2,1,0:T(8,128)(2,1)S(1)} collective-permute-done((bf16[4,32,2048]{2,1,0:T(8,128)(2,1)S(1)}, bf16[4,32,2048]{2,1,0:T(8,128)(2,1)S(1)}, u32[]{:S(2)}, u32[]{:S(2)}) %collective-permute-start.2) | collective-permute-done | bytes 524320 | tf_op jit(solution)/shard_map/ppermute | solution.py:22
  61.8 25.2 %collective-permute-done.3 = bf16[512,1024]{1,0:T(8,128)(2,1)S(1)} collective-permute-done((bf16[512,1024]{1,0:T(8,128)(2,1)S(1)}, bf16[512,1024]{1,0:T(8,128)(2,1)S(1)}, u32[]{:S(2)}, u32[]{:S(2)}) %collective-permute-start.3) | collective-permute-done | bytes 1048608 | tf_op jit(solution)/shard_map/ppermute | solution.py:22
  95.0 6.7 %collective-permute-done.6 = bf16[128,1024]{1,0:T(8,128)(2,1)} collective-permute-done((bf16[128,1024]{1,0:T(8,128)(2,1)S(1)}, bf16[128,1024]{1,0:T(8,128)(2,1)}, u32[]{:S(2)}, u32[]{:S(2)}) %collective-permute-start.6) | collective-permute-done | bytes 262176 | tf_op jit(solution)/shard_map/ppermute | solution.py:22
  109.5 7.9 %convolution_convert_fusion.1 = f16[1024,1024]{1,0:T(8,128)(2,1)} fusion(bf16[1024,2048]{1,0:T(8,128)(2,1)} %bitcast.9, bf16[512,1024]{1,0:T(8,128)(2,1)S(1)} %get-tuple-element.83, bf16[512,1024]{1,0:T(8,128)(2,1)S(1)} %get-tuple-element.84, bf16[512,1024]{1,0:T(8,128)(2,1)S(1)} %get-tuple-element.85, bf16[512,1024]{1,0:T(8,128)(2,1)S(1)} %get-tuple-element.82), kind=kOutput, calls=%fused_computation.14 | convolution fusion | flops 4312793088 | bytes 10485760 | tf_op jit(solution)/shard_map/dot_general | solution.py:102
  117.4 4.4 %all-gather.16.cloned.1.call-done = bf16[16,2,16,2048]{3,2,1,0:T(8,128)(2,1)} async-done(((bf16[4,2,16,2048]{3,2,1,0:T(8,128)(2,1)}), bf16[16,2,16,2048]{3,2,1,0:T(8,128)(2,1)}) %all-gather.16.cloned.1.call-update) | async-done | bytes 2097168 | tf_op jit(solution)/shard_map/all_gather | solution.py:97
  132.7 20.4 %all-to-all-done.1 = f16[4,256,1024]{2,1,0:T(8,128)(2,1)S(1)} async-done(((f16[4,256,1024]{2,1,0:T(8,128)(2,1)}), f16[4,256,1024]{2,1,0:T(8,128)(2,1)S(1)}, u32[]{:S(2)}, u32[]{:S(2)}) %all-to-all-start.1) | async-done | bytes 2097184 | tf_op jit(solution)/shard_map/all_to_all | solution.py:43
  160.8 5.7 %convolution_convert_fusion = f16[1024,1024]{1,0:T(8,128)(2,1)} fusion(bf16[1024,2048]{1,0:T(8,128)(2,1)S(1)} %bitcast.335, bf16[512,1024]{1,0:T(8,128)(2,1)S(1)} %copy-done.16, bf16[512,1024]{1,0:T(8,128)(2,1)S(1)} %copy-done.20, bf16[512,1024]{1,0:T(8,128)(2,1)S(1)} %copy-done.24, bf16[512,1024]{1,0:T(8,128)(2,1)S(1)} %copy-done.11), kind=kOutput, calls=%fused_computation.13 | convolution fusion | flops 4312793088 | bytes 10485760 | tf_op jit(solution)/shard_map/dot_general | solution.py:102
  181.0 15.4 %all-to-all-done.2 = f16[4,256,1024]{2,1,0:T(8,128)(2,1)S(1)} async-done(((f16[4,256,1024]{2,1,0:T(8,128)(2,1)}), f16[4,256,1024]{2,1,0:T(8,128)(2,1)S(1)}, u32[]{:S(2)}, u32[]{:S(2)}) %all-to-all-start.2) | async-done | bytes 2097184 | tf_op jit(solution)/shard_map/all_to_all | solution.py:43
  216.5 18.7 %all-gather.8.cloned.1.call-done = bf16[1024,1024]{1,0:T(8,128)(2,1)} async-done(((bf16[256,1024]{1,0:T(8,128)(2,1)}), bf16[1024,1024]{1,0:T(8,128)(2,1)}) %all-gather.8.cloned.1.call-update) | async-done | bytes 2097168 | tf_op jit(solution)/shard_map/all_gather | solution.py:121
  237.1 6.0 %multiply_convert_fusion.2 = f16[512,2048]{1,0:T(8,128)(2,1)} fusion(bf16[512,1024]{1,0:T(8,128)(2,1)S(1)} %bitcast.354, bf16[512,1024]{1,0:T(8,128)(2,1)} %copy-done.15, bf16[512,1024]{1,0:T(8,128)(2,1)} %copy-done.19, bf16[512,1024]{1,0:T(8,128)(2,1)} %copy-done.23, bf16[512,1024]{1,0:T(8,128)(2,1)} %copy-done.10), kind=kOutput, calls=%fused_computation.8 | convolution fusion | flops 2166358016 | bytes 7340032 | tf_op jit(solution)/shard_map/dot_general | solution.py:126
  256.9 6.3 %add_convert_fusion.1 = f16[512,2048]{1,0:T(8,128)(2,1)} fusion(f16[512,2048]{1,0:T(8,128)(2,1)} %collective-permute-done.24, bf16[512,1024]{1,0:T(8,128)(2,1)S(1)} %bitcast.353, bf16[512,1024]{1,0:T(8,128)(2,1)} %copy-done.15, bf16[512,1024]{1,0:T(8,128)(2,1)} %copy-done.19, bf16[512,1024]{1,0:T(8,128)(2,1)} %copy-done.23, bf16[512,1024]{1,0:T(8,128)(2,1)S(1)} %copy-done.12), kind=kOutput, calls=%fused_computation.7 | convolution fusion | flops 2168455168 | bytes 9437184 | tf_op jit(solution)/shard_map/dot_general | solution.py:126
  263.2 4.3 %all-to-all-start.3 = ((f16[4,4,32,2048]{3,2,1,0:T(8,128)(2,1)}), f16[4,4,32,2048]{3,2,1,0:T(8,128)(2,1)S(1)}, u32[]{:S(2)}, u32[]{:S(2)}) async-start(f16[4,4,32,2048]{3,2,1,0:T(8,128)(2,1)} %bitcast.344), calls=%async_computation.3 | async-start | bytes 4194304 | tf_op jit(solution)/shard_map/all_to_all | solution.py:43
  267.6 10.9 %fusion.103 = f32[2048,1024]{1,0:T(8,128)} fusion(bf16[1024,2048]{1,0:T(8,128)(2,1)} %bitcast.9, bf16[1024,1024]{1,0:T(8,128)(2,1)} %all-gather.8.cloned.1.call-done), kind=kOutput, calls=%fused_computation.295 | convolution fusion | flops 4294967296 | bytes 14680064 | tf_op jit(solution)/shard_map/dot_general | solution.py:130
  278.4 5.9 %all-gather.10.cloned.1.call-done = bf16[1024,1024]{1,0:T(8,128)(2,1)} async-done(((bf16[256,1024]{1,0:T(8,128)(2,1)}), bf16[1024,1024]{1,0:T(8,128)(2,1)}) %all-gather.10.cloned.1.call-update) | async-done | bytes 2097168 | tf_op jit(solution)/shard_map/all_gather | solution.py:121
  287.4 7.6 %multiply_convert_fusion.1 = f16[512,2048]{1,0:T(8,128)(2,1)} fusion(bf16[512,1024]{1,0:T(8,128)(2,1)S(1)} %bitcast.355, bf16[512,1024]{1,0:T(8,128)(2,1)S(1)} %copy-done.17, bf16[512,1024]{1,0:T(8,128)(2,1)S(1)} %copy-done.21, bf16[512,1024]{1,0:T(8,128)(2,1)S(1)} %copy-done.25, bf16[512,1024]{1,0:T(8,128)(2,1)S(1)} %copy-done.13), kind=kOutput, calls=%fused_computation.6 | convolution fusion | flops 2166358016 | bytes 7340032 | tf_op jit(solution)/shard_map/dot_general | solution.py:126
  302.4 7.2 %multiply_convert_fusion = f16[2048,1024]{1,0:T(8,128)(2,1)S(1)} fusion(f32[2048,1024]{1,0:T(8,128)} %fusion.103, bf16[1024,2048]{1,0:T(8,128)(2,1)S(1)} %bitcast.336, bf16[1024,1024]{1,0:T(8,128)(2,1)S(1)} %copy-done.7), kind=kOutput, calls=%fused_computation | convolution fusion | flops 4301258752 | bytes 18874368 | tf_op jit(solution)/shard_map/dot_general | solution.py:130
  315.3 9.0 %add_convert_fusion = f16[512,2048]{1,0:T(8,128)(2,1)} fusion(f16[512,2048]{1,0:T(8,128)(2,1)} %collective-permute-done.33, bf16[512,1024]{1,0:T(8,128)(2,1)S(1)} %bitcast.352, bf16[512,1024]{1,0:T(8,128)(2,1)S(1)} %copy-done.18, bf16[512,1024]{1,0:T(8,128)(2,1)S(1)} %copy-done.22, bf16[512,1024]{1,0:T(8,128)(2,1)S(1)} %copy-done.26, ...), kind=kOutput, calls=%fused_computation.5 | convolution fusion | flops 2168455168 | bytes 9437184 | tf_op jit(solution)/shard_map/dot_general | solution.py:126
  340.3 20.4 %collective-permute-done.32 = f16[512,1024]{1,0:T(8,128)(2,1)} collective-permute-done((f16[512,1024]{1,0:T(8,128)(2,1)}, f16[512,1024]{1,0:T(8,128)(2,1)}, u32[]{:S(2)}, u32[]{:S(2)}) %collective-permute-start.32) | collective-permute-done | bytes 1048608 | tf_op jit(solution)/shard_map/ppermute | solution.py:22
  368.0 4.6 %collective-permute-done.37 = f16[4,8,2048]{2,1,0:T(8,128)(2,1)S(1)} collective-permute-done((f16[4,8,2048]{2,1,0:T(8,128)(2,1)S(1)}, f16[4,8,2048]{2,1,0:T(8,128)(2,1)S(1)}, u32[]{:S(2)}, u32[]{:S(2)}) %collective-permute-start.37) | collective-permute-done | bytes 131104 | tf_op jit(solution)/shard_map/ppermute | solution.py:22
  398.2 4.4 %broadcast_in_dim.8 = f32[512,4096]{1,0:T(8,128)} broadcast(f32[]{:T(128)} %constant.208.clone.1), dimensions={} | broadcast | bytes 8388612 | tf_op jit(solution)/shard_map/broadcast_in_dim | solution.py:207
  411.5 9.0 %collective-permute-done.43 = bf16[18,8192]{1,0:T(8,128)(2,1)S(1)} collective-permute-done((bf16[18,8192]{1,0:T(8,128)(2,1)S(1)}, bf16[18,8192]{1,0:T(8,128)(2,1)S(1)}, u32[]{:S(2)}, u32[]{:S(2)}) %collective-permute-start.43) | collective-permute-done | bytes 294944 | tf_op jit(solution)/shard_map/ppermute | solution.py:15
  (351 shorter events, 180.8 us)
Async XLA Ops:
  8.8 14.9 %collective-permute-start = (bf16[32,8192]{1,0:T(8,128)(2,1)S(1)}, bf16[32,8192]{1,0:T(8,128)(2,1)S(1)}, u32[]{:S(2)}, u32[]{:S(2)}) collective-permute-start(bf16[32,8192]{1,0:T(8,128)(2,1)S(1)} %bitcast.331), channel_id=1, source_target_pairs={{0,64},{64,0},{1,65},{65,1},{2,66},{66,2},{3,67},{67,3},{4,68},{68... | collective-permute-start | bytes 1572872 | tf_op jit(solution)/shard_map/ppermute | solution.py:22
  12.1 30.9 %collective-permute-start.1 = (bf16[384,1024]{1,0:T(8,128)(2,1)S(1)}, bf16[384,1024]{1,0:T(8,128)(2,1)S(1)}, u32[]{:S(2)}, u32[]{:S(2)}) collective-permute-start(bf16[384,1024]{1,0:T(8,128)(2,1)S(1)} %constant_dynamic-slice_fusion), channel_id=1, source_target_pairs={{0,8},{4,12},{8,0},{12,4},{1,9},{5,13},{9,1},{13,5},{2,10},{6,14},... | collective-permute-start | bytes 2359304 | tf_op jit(solution)/shard_map/ppermute | solution.py:22
  27.4 15.6 %all-to-all-start = ((bf16[4,32,2048]{2,1,0:T(8,128)(2,1)}), bf16[4,32,2048]{2,1,0:T(8,128)(2,1)S(1)}, u32[]{:S(2)}, u32[]{:S(2)}) async-start(bf16[4,32,2048]{2,1,0:T(8,128)(2,1)} %copy.44), calls=%async_computation | async-start | bytes 1048576 | tf_op jit(solution)/shard_map/all_to_all | solution.py:43
  32.0 56.5 %all-gather.14.cloned.1.call-start = ((), (), s32[]{:S(2)}) async-start(), calls=%async_computation.8 | async-start | bytes 2621440 | tf_op jit(solution)/shard_map/all_gather | solution.py:97
  58.6 63.2 %all-gather.16.cloned.1.call-start = ((), (), s32[]{:S(2)}) async-start(), calls=%async_computation.9 | async-start | bytes 2621440 | tf_op jit(solution)/shard_map/all_gather | solution.py:97
  61.8 25.2 %collective-permute-start.3 = (bf16[512,1024]{1,0:T(8,128)(2,1)S(1)}, bf16[512,1024]{1,0:T(8,128)(2,1)S(1)}, u32[]{:S(2)}, u32[]{:S(2)}) collective-permute-start(bf16[512,1024]{1,0:T(8,128)(2,1)S(1)} %get-tuple-element.30), channel_id=1, source_target_pairs={{0,12},{4,8},{8,4},{12,0},{1,13},{5,9},{9,5},{13,1},{2,14},{6,10},... | collective-permute-start | bytes 3145736 | tf_op jit(solution)/shard_map/ppermute | solution.py:22
  88.5 16.9 %collective-permute-start.4 = (bf16[4,4,2,16,2048]{4,3,2,1,0:T(8,128)(2,1)}, bf16[4,4,2,16,2048]{4,3,2,1,0:T(8,128)(2,1)S(1)}, u32[]{:S(2)}, u32[]{:S(2)}) collective-permute-start(bf16[4,4,2,16,2048]{4,3,2,1,0:T(8,128)(2,1)} %bitcast.349), channel_id=1, source_target_pairs={{0,4},{4,0},{1,5},{5,1},{2,6},{6,2},{3,7},{7,3},{8,12},{12,8},{9,1... | collective-permute-start | bytes 6291464 | tf_op jit(solution)/shard_map/ppermute | solution.py:22
  88.5 14.5 %collective-permute-start.5 = (bf16[512,1024]{1,0:T(8,128)(2,1)}, bf16[512,1024]{1,0:T(8,128)(2,1)}, u32[]{:S(2)}, u32[]{:S(2)}) collective-permute-start(bf16[512,1024]{1,0:T(8,128)(2,1)} %get-tuple-element.88), channel_id=1, source_target_pairs={{0,4},{4,0},{8,12},{12,8},{1,5},{5,1},{9,13},{13,9},{2,6},{6,2},{1... | collective-permute-start | bytes 3145736 | tf_op jit(solution)/shard_map/ppermute | solution.py:22
  121.8 32.2 %collective-permute-start.13 = (bf16[4,4,2,16,2048]{4,3,2,1,0:T(8,128)(2,1)}, bf16[4,4,2,16,2048]{4,3,2,1,0:T(8,128)(2,1)}, u32[]{:S(2)}, u32[]{:S(2)}) collective-permute-start(bf16[4,4,2,16,2048]{4,3,2,1,0:T(8,128)(2,1)} %bitcast.347), channel_id=1, source_target_pairs={{0,4},{4,0},{1,5},{5,1},{2,6},{6,2},{3,7},{7,3},{8,12},{12,8},{9,1... | collective-permute-start | bytes 6291464 | tf_op jit(solution)/shard_map/ppermute | solution.py:22
  121.8 31.3 %all-to-all-start.1 = ((f16[4,256,1024]{2,1,0:T(8,128)(2,1)}), f16[4,256,1024]{2,1,0:T(8,128)(2,1)S(1)}, u32[]{:S(2)}, u32[]{:S(2)}) async-start(f16[4,256,1024]{2,1,0:T(8,128)(2,1)} %bitcast.343), calls=%async_computation.1 | async-start | bytes 4194304 | tf_op jit(solution)/shard_map/all_to_all | solution.py:43
  166.5 29.9 %all-to-all-start.2 = ((f16[4,256,1024]{2,1,0:T(8,128)(2,1)}), f16[4,256,1024]{2,1,0:T(8,128)(2,1)S(1)}, u32[]{:S(2)}, u32[]{:S(2)}) async-start(f16[4,256,1024]{2,1,0:T(8,128)(2,1)} %bitcast.341), calls=%async_computation.2 | async-start | bytes 4194304 | tf_op jit(solution)/shard_map/all_to_all | solution.py:43
  170.2 65.0 %all-gather.8.cloned.1.call-start = ((), (), s32[]{:S(2)}) async-start(), calls=%async_computation.5 | async-start | bytes 2621440 | tf_op jit(solution)/shard_map/all_gather | solution.py:121
  204.5 79.8 %all-gather.10.cloned.1.call-start = ((), (), s32[]{:S(2)}) async-start(), calls=%async_computation.6 | async-start | bytes 2621440 | tf_op jit(solution)/shard_map/all_gather | solution.py:121
  263.2 31.8 %all-to-all-start.3 = ((f16[4,4,32,2048]{3,2,1,0:T(8,128)(2,1)}), f16[4,4,32,2048]{3,2,1,0:T(8,128)(2,1)S(1)}, u32[]{:S(2)}, u32[]{:S(2)}) async-start(f16[4,4,32,2048]{3,2,1,0:T(8,128)(2,1)} %bitcast.344), calls=%async_computation.3 | async-start | bytes 4194304 | tf_op jit(solution)/shard_map/all_to_all | solution.py:43
  295.0 20.2 %collective-permute-start.33 = (f16[512,2048]{1,0:T(8,128)(2,1)}, f16[512,2048]{1,0:T(8,128)(2,1)}, u32[]{:S(2)}, u32[]{:S(2)}) collective-permute-start(f16[512,2048]{1,0:T(8,128)(2,1)} %multiply_convert_fusion.1), channel_id=1, source_target_pairs={{0,4},{4,0},{1,5},{5,1},{2,6},{6,2},{3,7},{7,3},{8,12},{12,8},{9,1... | collective-permute-start | bytes 6291464 | tf_op jit(solution)/shard_map/ppermute | solution.py:22
  295.9 16.4 %collective-permute-start.26 = (f16[4,8,2048]{2,1,0:T(8,128)(2,1)S(1)}, f16[4,8,2048]{2,1,0:T(8,128)(2,1)S(1)}, u32[]{:S(2)}, u32[]{:S(2)}) collective-permute-start(f16[4,8,2048]{2,1,0:T(8,128)(2,1)S(1)} %get-tuple-element.111), channel_id=1, source_target_pairs={{0,64},{8,72},{64,0},{72,8},{1,65},{9,73},{65,1},{73,9},{2,66},{10... | collective-permute-start | bytes 393224 | tf_op jit(solution)/shard_map/ppermute | solution.py:22
  297.5 14.8 %collective-permute-start.27 = (f16[4,8,2048]{2,1,0:T(8,128)(2,1)S(1)}, f16[4,8,2048]{2,1,0:T(8,128)(2,1)S(1)}, u32[]{:S(2)}, u32[]{:S(2)}) collective-permute-start(f16[4,8,2048]{2,1,0:T(8,128)(2,1)S(1)} %get-tuple-element.112), channel_id=1, source_target_pairs={{0,72},{8,64},{64,8},{72,0},{1,73},{9,65},{65,9},{73,1},{2,74},{10... | collective-permute-start | bytes 393224 | tf_op jit(solution)/shard_map/ppermute | solution.py:22
  312.3 27.9 %collective-permute-start.31 = (f16[512,1024]{1,0:T(8,128)(2,1)}, f16[512,1024]{1,0:T(8,128)(2,1)}, u32[]{:S(2)}, u32[]{:S(2)}) collective-permute-start(f16[512,1024]{1,0:T(8,128)(2,1)} %get-tuple-element.42), channel_id=1, source_target_pairs={{0,8},{4,12},{8,0},{12,4},{1,9},{5,13},{9,1},{13,5},{2,10},{6,14},... | collective-permute-start | bytes 3145736 | tf_op jit(solution)/shard_map/ppermute | solution.py:22
  315.2 45.4 %collective-permute-start.32 = (f16[512,1024]{1,0:T(8,128)(2,1)}, f16[512,1024]{1,0:T(8,128)(2,1)}, u32[]{:S(2)}, u32[]{:S(2)}) collective-permute-start(f16[512,1024]{1,0:T(8,128)(2,1)} %get-tuple-element.43), channel_id=1, source_target_pairs={{0,12},{4,8},{8,4},{12,0},{1,13},{5,9},{9,5},{13,1},{2,14},{6,10},... | collective-permute-start | bytes 3145736 | tf_op jit(solution)/shard_map/ppermute | solution.py:22
  324.3 36.4 %all-to-all-start.4 = ((f16[4,4,32,2048]{3,2,1,0:T(8,128)(2,1)}), f16[4,4,32,2048]{3,2,1,0:T(8,128)(2,1)S(1)}, u32[]{:S(2)}, u32[]{:S(2)}) async-start(f16[4,4,32,2048]{3,2,1,0:T(8,128)(2,1)} %bitcast.342), calls=%async_computation.4 | async-start | bytes 4194304 | tf_op jit(solution)/shard_map/all_to_all | solution.py:43
  328.5 92.9 %all-gather.12.cloned.1.call-start = ((), (), s32[]{:S(2)}) async-start(), calls=%async_computation.7 | async-start | bytes 1310720 | tf_op jit(solution)/shard_map/all_gather | solution.py:196
  392.5 18.9 %collective-permute-start.44 = (bf16[18,8192]{1,0:T(8,128)(2,1)S(1)}, bf16[18,8192]{1,0:T(8,128)(2,1)S(1)}, u32[]{:S(2)}, u32[]{:S(2)}) collective-permute-start(bf16[18,8192]{1,0:T(8,128)(2,1)S(1)} %pad_maximum_fusion.5), channel_id=1, source_target_pairs={{3,0},{0,1},{1,2},{2,3},{7,4},{4,5},{5,6},{6,7},{11,8},{8,9},{9,10... | collective-permute-start | bytes 884744 | tf_op jit(solution)/shard_map/ppermute | solution.py:15
  394.1 26.3 %collective-permute-start.43 = (bf16[18,8192]{1,0:T(8,128)(2,1)S(1)}, bf16[18,8192]{1,0:T(8,128)(2,1)S(1)}, u32[]{:S(2)}, u32[]{:S(2)}) collective-permute-start(bf16[18,8192]{1,0:T(8,128)(2,1)S(1)} %pad_maximum_fusion.5), channel_id=1, source_target_pairs={{2,0},{3,1},{0,2},{1,3},{6,4},{7,5},{4,6},{5,7},{10,8},{11,9},{8,1... | collective-permute-start | bytes 884744 | tf_op jit(solution)/shard_map/ppermute | solution.py:15
  396.8 23.7 %collective-permute-start.42 = (bf16[18,8192]{1,0:T(8,128)(2,1)S(1)}, bf16[18,8192]{1,0:T(8,128)(2,1)S(1)}, u32[]{:S(2)}, u32[]{:S(2)}) collective-permute-start(bf16[18,8192]{1,0:T(8,128)(2,1)S(1)} %pad_maximum_fusion.5), channel_id=1, source_target_pairs={{1,0},{2,1},{3,2},{0,3},{5,4},{6,5},{7,6},{4,7},{9,8},{10,9},{11,1... | collective-permute-start | bytes 884744 | tf_op jit(solution)/shard_map/ppermute | solution.py:15
  (70 other events, 487.2 us)
Sparse Core Ops, SparseCore 0:
  58.7 29.6 all-gather.13
  90.9 30.8 all-gather.15
  204.6 30.5 all-gather.7
  253.7 30.5 all-gather.9
  386.2 34.8 all-gather.11
